TPU v7x, 32 devices: a whole 2x2x4 slice. The times are simulated.
32 devices in a mesh: rep: 2 (over x), tp: 16 (over z, y, core).
Axes of the slice: x: 2, y: 2, z: 4, core: 2. Of those that a mesh axis runs over, the one named last changes fastest.
Arguments:
- tokens: bfloat16 [2, 512, 4096], P(None, 'rep', 'tp'), parts along dimension 1, may hold values from -640 to 640, as said below
- prenorm_gain: bfloat16 [4096], replicated, may hold values from 0.099609375 to 1.8984375
- gate_matrix: bfloat16 [4096, 16384], P(None, 'tp'), may hold values from -0.09375 to 0.09375
- up_weight: bfloat16 [4096, 16384], P(None, 'tp'), may hold values from -0.09375 to 0.09375
- down_weight: bfloat16 [16384, 4096], P('tp'), may hold values from -0.0625 to 0.0625
- a_store: bfloat16 [128, 16, 16384], P('tp'), may hold values from -0.046875 to 0.046875
- b_store: bfloat16 [128, 16, 4096], P('tp'), may hold values from -1.5 to 1.5
- adapter_slot: int32 [256], P('rep'), parts along dimension 0, may hold values from 0 to 127, as said below
- row_adapter: int32 [512], P('rep'), parts along dimension 0, may hold values from 0 to 127, as said below
Outputs:
- mixed: bfloat16 [4096, 2, 512], P('tp', None, 'rep'), parts along dimension 2
There are 2 independent parts, one for each index of `rep`. A program takes and returns all parts, laid end to end along the dimension named above; an argument that names none is the same for every part. Nothing has to cross between parts.
Inputs may be any that keep to these rules, and one draw needn't show every extreme that they name: A permutation: adapter a is stored at index adapter_slot[a] of a_store and b_store, which lies on device adapter_slot[a] // 8 of tp. `row_adapter`: Nondecreasing. Of the adapters that the requests name, at most 2 are stored on one device, and on some device exactly 2. `tokens`: rows and features of different scale.
All inputs are finite; a program needn't handle non-finite values.
Results may differ from a plain program's by a relative error of at most 0.0069.
Values may be sent and summed in bfloat16 or wider, within the bound.
A program may use at most 192 MiB of HBM per device.

v0:
```python
import jax
import jax.numpy as jnp
from jax import lax
from jax.sharding import PartitionSpec as P

EPS = 1e-06
ADAPTER_SCALING = 2.0


def body(
    tokens,
    prenorm_gain,
    gate_matrix,
    up_weight,
    down_weight,
    a_store,
    b_store,
    adapter_slot,
    row_adapter,
):
    whole = lax.all_gather(tokens, "tp", axis=2, tiled=True)
    steps_count, rows_count, width = whole.shape
    total_rows = steps_count * rows_count
    flat = whole.reshape(total_rows, width).astype(jnp.float32)
    scale = lax.rsqrt(jnp.mean(flat * flat, axis=1, keepdims=True) + EPS)
    normed = (flat * scale * prenorm_gain.astype(jnp.float32)).astype(jnp.bfloat16)
    gate = jnp.dot(normed, gate_matrix, preferred_element_type=jnp.float32)
    up = jnp.dot(normed, up_weight, preferred_element_type=jnp.float32)
    hidden = (jax.nn.silu(gate) * up).astype(jnp.bfloat16)
    held = a_store.shape[0]
    rank_count = a_store.shape[1]
    groups = lax.axis_size("tp")
    myself = lax.axis_index("tp")
    stored = groups * held
    catalog = jnp.arange(stored, dtype=jnp.int32)
    matches = row_adapter[:, None] == catalog[None, :]
    row_slot = jnp.sum(jnp.where(matches, adapter_slot[None, :], 0), axis=1)
    got_a, got_b = (
        lax.all_to_all(a_store, "tp", split_axis=2, concat_axis=0, tiled=True),
        lax.all_to_all(b_store, "tp", split_axis=2, concat_axis=0, tiled=True),
    )
    place_all = jnp.tile(row_slot, steps_count)
    slot_count = got_a.shape[0]
    chooser = jnp.arange(slot_count, dtype=jnp.int32)[:, None] == place_all[None, :]
    first_flat = got_a.reshape(slot_count * rank_count, got_a.shape[2])
    every_shrink = lax.dot_general(
        first_flat, hidden, (((1,), (1,)), ((), ())), preferred_element_type=jnp.float32
    )
    every_shrink = every_shrink.reshape(slot_count, rank_count, total_rows)
    shrink = jnp.sum(jnp.where(chooser[:, None, :], every_shrink, 0.0), axis=0)
    piece = width // groups
    base_output = lax.dot_general(
        down_weight, hidden, (((0,), (1,)), ((), ())), preferred_element_type=jnp.float32
    )
    base_output, shrink = lax.psum((base_output, shrink), "tp")
    base_output = lax.dynamic_slice_in_dim(base_output, myself * piece, piece, 0)
    shrink_low = shrink.astype(jnp.bfloat16)
    spread = jnp.where(chooser[:, None, :], shrink_low[None, :, :], jnp.zeros((), jnp.bfloat16))
    spread = spread.reshape(slot_count * rank_count, total_rows)
    second_flat = got_b.reshape(slot_count * rank_count, got_b.shape[2])
    adapter_delta = lax.dot_general(
        second_flat, spread, (((0,), (0,)), ((), ())), preferred_element_type=jnp.float32
    )
    mixed = (base_output + ADAPTER_SCALING * adapter_delta).astype(jnp.bfloat16)
    return mixed.reshape(piece, steps_count, rows_count)


def solution(mesh):
    placed = (
        P(None, "rep", "tp"),
        P(),
        P(None, "tp"),
        P(None, "tp"),
        P("tp", None),
        P("tp", None, None),
        P("tp", None, None),
        P("rep"),
        P("rep"),
    )
    return jax.shard_map(
        body, mesh=mesh, in_specs=placed, out_specs=P("tp", None, "rep"), check_vma=False
    )
```

profile of v0, /device:TPU:0, one launch (start us, length us, event | category | flops | bytes accessed | tf_op | source)
XLA Modules:
  0.0 380.2 jit_solution(16511674017201354982)
XLA Ops:
  6.5 0.7 all-gather.2.cloned.1.call-update
  7.3 8.2 %copy.29 = bf16[8,16,4096]{1,0,2:T(8,128)(2,1)} copy(bf16[8,16,4096]{2,1,0:T(8,128)(2,1)} %param.15) | data formatting | bytes 2097152 | tf_op args[6]
  15.5 11.3 %reshape.79 = bf16[16,2,16384]{2,1,0:T(2,128)(2,1)} reshape(bf16[4096,8,16]{2,1,0:T(8,128)(2,1)} %bitcast.52) | data formatting | bytes 2097152
  26.8 7.4 %all-to-all-start.1 = ((bf16[16,2,16384]{2,1,0:T(2,128)(2,1)}), bf16[16,2,16384]{2,1,0:T(2,128)(2,1)S(1)}, u32[]{:S(2)}, u32[]{:S(2)}) async-start(bf16[16,2,16384]{2,1,0:T(2,128)(2,1)} %reshape.79), calls=%async_computation.1 | async-start | bytes 2097152 | tf_op jit(solution)/shard_map/all_to_all | solution.py:40
  34.2 27.2 %copy.25 = bf16[8,16,16384]{1,0,2:T(8,128)(2,1)} copy(bf16[8,16,16384]{2,1,0:T(8,128)(2,1)} %param.14) | data formatting | bytes 8388608 | tf_op args[5]
  61.5 37.0 %reshape.77 = bf16[16,2,65536]{2,1,0:T(2,128)(2,1)} reshape(bf16[16384,8,16]{2,1,0:T(8,128)(2,1)} %bitcast.50) | data formatting | bytes 8388608
  98.5 3.1 multiply_reduce_fusion
  101.6 5.9 %all-to-all-start = ((bf16[16,2,65536]{2,1,0:T(2,128)(2,1)}), bf16[16,2,65536]{2,1,0:T(2,128)(2,1)}, u32[]{:S(2)}, u32[]{:S(2)}) async-start(bf16[16,2,65536]{2,1,0:T(2,128)(2,1)} %reshape.77), calls=%async_computation | async-start | bytes 8388608 | tf_op jit(solution)/shard_map/all_to_all | solution.py:39
  107.6 4.0 %fusion.1 = bf16[512,4096]{1,0:T(8,128)(2,1)S(1)} fusion(f32[4096]{0:T(1024)S(1)} %convert_element_type.27, f32[512]{0:T(512)S(1)} %bitcast.58, bf16[2,256,4096]{2,1,0:T(8,128)(2,1)} %all-gather.2.cloned.1.call-done), kind=kLoop, calls=%fused_computation.2 | loop fusion | flops 8388608 | bytes 8407040 | tf_op jit(solution)/shard_map/convert_element_type | solution.py:26
  111.6 7.3 %fusion.5 = f32[512,1024]{1,0:T(8,128)S(1)} fusion(bf16[512,4096]{1,0:T(8,128)(2,1)S(1)} %fusion.1, bf16[4096,1024]{1,0:T(8,128)(2,1)} %param.11), kind=kOutput, calls=%fused_computation.18 | convolution fusion | flops 4294967296 | bytes 14680064 | tf_op jit(solution)/shard_map/dot_general | solution.py:27
  118.9 4.7 %multiply_convert_fusion = bf16[512,1024]{1,0:T(8,128)(2,1)S(1)} fusion(f32[512,1024]{1,0:T(8,128)S(1)} %fusion.5, bf16[512,4096]{1,0:T(8,128)(2,1)S(1)} %fusion.1, bf16[4096,1024]{1,0:T(8,128)(2,1)S(1)} %bitcast.61), kind=kOutput, calls=%fused_computation.7 | convolution fusion | flops 4298113024 | bytes 15728640 | tf_op jit(solution)/shard_map/dot_general | solution.py:28
  123.6 1.0 copy-done.3
  124.6 6.8 %convolution_bitcast_fusion = f32[4096,512]{0,1:T(8,128)} fusion(bf16[512,1024]{1,0:T(8,128)(2,1)S(1)} %multiply_convert_fusion, bf16[1024,4096]{1,0:T(8,128)(2,1)S(1)} %bitcast.63), kind=kOutput, calls=%fused_computation.4 | convolution fusion | flops 4294967296 | bytes 17825792 | tf_op jit(solution)/shard_map/dot_general | solution.py:52
  132.3 7.6 %reshape.80 = bf16[4096,8,16]{2,1,0:T(8,128)(2,1)} reshape(bf16[16,2,16384]{2,1,0:T(2,128)(2,1)S(1)} %all-to-all-done.1) | data formatting | bytes 2097152
  139.9 7.5 %copy.31 = bf16[16,8,16,256]{3,2,1,0:T(8,128)(2,1)S(1)} copy(bf16[16,8,16,256]{2,1,3,0:T(8,128)(2,1)} %bitcast.51) | data formatting | bytes 2097152 | tf_op jit(solution)/shard_map/all_to_all | solution.py:40
  147.3 67.4 %all-to-all-done = bf16[16,2,65536]{2,1,0:T(2,128)(2,1)} async-done(((bf16[16,2,65536]{2,1,0:T(2,128)(2,1)}), bf16[16,2,65536]{2,1,0:T(2,128)(2,1)}, u32[]{:S(2)}, u32[]{:S(2)}) %all-to-all-start) | async-done | bytes 4194336 | tf_op jit(solution)/shard_map/all_to_all | solution.py:39
  214.7 25.6 %reshape.78 = bf16[16384,8,16]{2,1,0:T(8,128)(2,1)} reshape(bf16[16,2,65536]{2,1,0:T(2,128)(2,1)} %all-to-all-done) | data formatting | bytes 8388608
  240.3 33.1 %copy.27 = bf16[16,8,16,1024]{3,2,1,0:T(8,128)(2,1)} copy(bf16[16,8,16,1024]{2,1,3,0:T(8,128)(2,1)} %bitcast.49) | data formatting | bytes 8388608 | tf_op jit(solution)/shard_map/all_to_all | solution.py:39
  273.4 6.5 %convolution_bitcast_fusion.1 = f32[2048,512]{0,1:T(8,128)} fusion(bf16[512,1024]{1,0:T(8,128)(2,1)S(1)} %copy-done.4, bf16[2048,1024]{1,0:T(8,128)(2,1)} %bitcast.54), kind=kOutput, calls=%fused_computation.6 | convolution fusion | flops 2147483648 | bytes 9437184 | tf_op jit(solution)/shard_map/dot_general | solution.py:46
  279.9 5.5 %copy.28 = f32[2048,512]{1,0:T(8,128)} copy(f32[2048,512]{0,1:T(8,128)} %convolution_bitcast_fusion.1) | data formatting | bytes 8388608 | tf_op jit(solution)/shard_map/dot_general | solution.py:46
  285.4 2.9 select_reduce_fusion
  288.2 82.1 %psum.15 = bf16[16,512]{1,0:T(8,128)(2,1)S(1)} all-reduce(f32[16,512]{1,0:T(8,128)S(1)} %select_reduce_fusion), channel_id=1, replica_groups=mesh['rep'=2,'tp'=16] {'tp'}, use_global_device_ids=true, to_apply=%region_4.5 | all-reduce | flops 8192 | bytes 49152 | tf_op jit(solution)/shard_map/psum | solution.py:55
  370.7 1.8 fusion.4
  372.5 0.9 copy.32
  (33 shorter events, 1.3 us)
Async XLA Ops:
  6.5 91.9 %all-gather.2.cloned.1.call-start = ((), (), s32[]{:S(2)}) async-start(), calls=%async_computation.2 | async-start | bytes 4456448 | tf_op jit(solution)/shard_map/all_gather | solution.py:21
  15.5 18.7 %copy-start = (bf16[4096]{0:T(1024)(128)(2,1)S(1)}, bf16[4096]{0:T(1024)(128)(2,1)}, u32[]{:S(2)}) copy-start(bf16[4096]{0:T(1024)(128)(2,1)} %param.10) | copy-start | bytes 24580
  26.8 74.8 %all-to-all-start.1 = ((bf16[16,2,16384]{2,1,0:T(2,128)(2,1)}), bf16[16,2,16384]{2,1,0:T(2,128)(2,1)S(1)}, u32[]{:S(2)}, u32[]{:S(2)}) async-start(bf16[16,2,16384]{2,1,0:T(2,128)(2,1)} %reshape.79), calls=%async_computation.1 | async-start | bytes 2097152 | tf_op jit(solution)/shard_map/all_to_all | solution.py:40
  101.6 113.1 %all-to-all-start = ((bf16[16,2,65536]{2,1,0:T(2,128)(2,1)}), bf16[16,2,65536]{2,1,0:T(2,128)(2,1)}, u32[]{:S(2)}, u32[]{:S(2)}) async-start(bf16[16,2,65536]{2,1,0:T(2,128)(2,1)} %reshape.77), calls=%async_computation | async-start | bytes 8388608 | tf_op jit(solution)/shard_map/all_to_all | solution.py:39
  107.5 263.2 %all-reduce.2.cloned.1.call-start = ((), (), s32[]{:S(2)}) async-start(), calls=%async_computation.3 | async-start | bytes 16777216 | tf_op jit(solution)/shard_map/psum | solution.py:55
  107.5 11.3 %slice-start = ((s8[8388608]{0:T(1024)(128)(4,1)}), s8[4194304]{0:T(1024)(128)(4,1)S(1)}, s32[]{:S(2)}) async-start(s8[8388608]{0:T(1024)(128)(4,1)} %bitcast.60), calls=%async_computation.4 | async-start | bytes 8388608
  107.6 17.0 %slice-start.2 = ((s8[8388608]{0:T(1024)(128)(4,1)}), s8[4194304]{0:T(1024)(128)(4,1)S(1)}, s32[]{:S(2)}) async-start(s8[8388608]{0:T(1024)(128)(4,1)} %bitcast.62), calls=%async_computation.6 | async-start | bytes 8388608
  111.5 7.3 %slice-start.1 = ((s8[8388608]{0:T(1024)(128)(4,1)}), s8[4194304]{0:T(1024)(128)(4,1)S(1)}, s32[]{:S(2)}) async-start(s8[8388608]{0:T(1024)(128)(4,1)} %bitcast.60), calls=%async_computation.5 | async-start | bytes 8388608
  111.6 13.0 %slice-start.3 = ((s8[8388608]{0:T(1024)(128)(4,1)}), s8[4194304]{0:T(1024)(128)(4,1)S(1)}, s32[]{:S(2)}) async-start(s8[8388608]{0:T(1024)(128)(4,1)} %bitcast.62), calls=%async_computation.7 | async-start | bytes 8388608
  123.6 1.0 copy-start.3
  131.4 0.7 copy-start.1
  131.4 0.7 copy-start.2
  240.3 33.1 %copy-start.4 = (bf16[512,1024]{1,0:T(8,128)(2,1)S(1)}, bf16[512,1024]{1,0:T(8,128)(2,1)}, u32[]{:S(2)}) copy-start(bf16[512,1024]{1,0:T(8,128)(2,1)} %copy-done.3) | copy-start | bytes 3145732
Sparse Core Ops, SparseCore 0:
  9.5 70.3 all-gather.1
  131.5 231.2 all-reduce.1
where the time goes:
time: 383 us; the launch traced here: 380 us
  local copies, waits for them, and re-layouts  165 us (43%)
  blocking collectives  82.1 us (21%)
  waiting for transfers between devices  68.1 us (18%)
  matrix products  27.1 us (7%)
  between operations  13.6 us (4%)
  starting transfers between devices  13.4 us (3%)
  other arithmetic  10.5 us (3%)
    unnamed x27, local copies, waits for them, and re-layouts  119 us
    psum x1, blocking collectives, body(): base_output, shrink = lax.psum((base_output, shrink), 'tp')  82.1 us
    all_to_all x1, waiting for transfers between devices, body(): lax.all_to_all(a_store, 'tp', split_axis=2, concat_axis=0, tiled=True)  67.4 us
    all_to_all x1, local copies, waits for them, and re-layouts, body(): lax.all_to_all(a_store, 'tp', split_axis=2, concat_axis=0, tiled=True)  33.1 us
  transfers between devices with their start and end apart: 4, of which 1 were waited for; matrix products, arithmetic and copies ran while one was open for 52% of the time, Pallas kernels for 0%

commit v1 on v0

--- a/solution.py
+++ b/solution.py
@@ -5,6 +5,7 @@
 
 EPS = 1e-06
 ADAPTER_SCALING = 2.0
+MOST = 2
 
 
 def body(
@@ -18,6 +19,33 @@
     adapter_slot,
     row_adapter,
 ):
+    held, rank_count, hidden_all = a_store.shape
+    groups = lax.axis_size("tp")
+    myself = lax.axis_index("tp")
+    stored = groups * held
+    catalog = jnp.arange(stored, dtype=jnp.int32)
+    matches = row_adapter[:, None] == catalog[None, :]
+    row_slot = jnp.sum(jnp.where(matches, adapter_slot[None, :], 0), axis=1)
+
+    home = row_slot // held
+    local = row_slot - home * held
+    at_home = home[None, :] == jnp.arange(groups, dtype=jnp.int32)[:, None]
+    lowest = jnp.min(jnp.where(at_home, local[None, :], held - 1), axis=1)
+    highest = jnp.max(jnp.where(at_home, local[None, :], 0), axis=1)
+    row_lowest = jnp.sum(jnp.where(at_home, lowest[:, None], 0), axis=0)
+    compact = home * MOST + (local != row_lowest).astype(jnp.int32)
+    mine_low = lax.dynamic_index_in_dim(lowest, myself, 0, False)
+    mine_high = lax.dynamic_index_in_dim(highest, myself, 0, False)
+
+    def chosen(store):
+        return jnp.concatenate(
+            [
+                lax.dynamic_slice_in_dim(store, mine_low, 1, 0),
+                lax.dynamic_slice_in_dim(store, mine_high, 1, 0),
+            ],
+            axis=0,
+        )
+
     whole = lax.all_gather(tokens, "tp", axis=2, tiled=True)
     steps_count, rows_count, width = whole.shape
     total_rows = steps_count * rows_count
@@ -27,19 +55,10 @@
     gate = jnp.dot(normed, gate_matrix, preferred_element_type=jnp.float32)
     up = jnp.dot(normed, up_weight, preferred_element_type=jnp.float32)
     hidden = (jax.nn.silu(gate) * up).astype(jnp.bfloat16)
-    held = a_store.shape[0]
-    rank_count = a_store.shape[1]
-    groups = lax.axis_size("tp")
-    myself = lax.axis_index("tp")
-    stored = groups * held
-    catalog = jnp.arange(stored, dtype=jnp.int32)
-    matches = row_adapter[:, None] == catalog[None, :]
-    row_slot = jnp.sum(jnp.where(matches, adapter_slot[None, :], 0), axis=1)
-    got_a, got_b = (
-        lax.all_to_all(a_store, "tp", split_axis=2, concat_axis=0, tiled=True),
-        lax.all_to_all(b_store, "tp", split_axis=2, concat_axis=0, tiled=True),
-    )
-    place_all = jnp.tile(row_slot, steps_count)
+
+    got_a = lax.all_to_all(chosen(a_store), "tp", split_axis=2, concat_axis=0, tiled=True)
+    got_b = lax.all_to_all(chosen(b_store), "tp", split_axis=2, concat_axis=0, tiled=True)
+    place_all = jnp.tile(compact, steps_count)
     slot_count = got_a.shape[0]
     chooser = jnp.arange(slot_count, dtype=jnp.int32)[:, None] == place_all[None, :]
     first_flat = got_a.reshape(slot_count * rank_count, got_a.shape[2])
@@ -48,12 +67,14 @@
     )
     every_shrink = every_shrink.reshape(slot_count, rank_count, total_rows)
     shrink = jnp.sum(jnp.where(chooser[:, None, :], every_shrink, 0.0), axis=0)
+    shrink = lax.psum(shrink, "tp")
     piece = width // groups
     base_output = lax.dot_general(
         down_weight, hidden, (((0,), (1,)), ((), ())), preferred_element_type=jnp.float32
     )
-    base_output, shrink = lax.psum((base_output, shrink), "tp")
-    base_output = lax.dynamic_slice_in_dim(base_output, myself * piece, piece, 0)
+    base_output = lax.psum_scatter(
+        base_output.astype(jnp.bfloat16), "tp", scatter_dimension=0, tiled=True
+    ).astype(jnp.float32)
     shrink_low = shrink.astype(jnp.bfloat16)
     spread = jnp.where(chooser[:, None, :], shrink_low[None, :, :], jnp.zeros((), jnp.bfloat16))
     spread = spread.reshape(slot_count * rank_count, total_rows)

time: 383 us -> 264 us (0.69)
  local copies, waits for them, and re-layouts: 165 us -> 64.7 us
  blocking collectives: 82.1 us -> 65.4 us
  waiting for transfers between devices: 68.1 us -> 78.1 us
  matrix products: 27.1 us -> 20.7 us
  starting transfers between devices: 13.4 us -> 9.52 us
    unnamed x27 -> x19, local copies, waits for them, and re-layouts: 119 us -> 26.1 us
    all_gather x1, waiting for transfers between devices: 0.01 us -> 50.4 us  [body(): whole = lax.all_gather(tokens, 'tp', axis=2, tiled=True)]
    all_to_all x2, waiting for transfers between devices: 67.4 us -> 26.9 us  [the longest x1 26.9 us: body(): lax.all_to_all(chosen(a_store), 'tp', split_axis=2, concat_axis=0, tiled=...]
    all_to_all x2, local copies, waits for them, and re-layouts: 40.6 us -> 18.9 us  [the longest x1 17.8 us: body(): lax.all_to_all(chosen(a_store), 'tp', split_axis=2, concat_axis=0, tiled=...]
    psum x1, blocking collectives: 82.1 us -> 65.4 us  [body(): shrink = lax.psum(shrink, 'tp')]
    concatenate x0 -> x2, local copies, waits for them, and re-layouts: none -> 15.4 us  [chosen(): jnp.concatenate([lax.dynamic_slice_in_dim(store, mine_low, 1, 0), lax.dyn...]
    dot_general x1, matrix products: 6.51 us -> 0.74 us  [body(): lax.dot_general(first_flat, hidden, (((1,), (1,)), ((), ())), preferred_e...]
    dot_general x1 -> x0, local copies, waits for them, and re-layouts: 5.45 us -> none  [body(): lax.dot_general(first_flat, hidden, (((1,), (1,)), ((), ())), preferred_e...]
  transfers between devices with their start and end apart: 4 -> 4, of which waited for: 1 -> 2; matrix products, arithmetic and copies ran while one was open for 52% -> 24% of each run, Pallas kernels for 0% -> 0%
where the time goes in v1:
time: 264 us; the launch traced here: 263 us
  waiting for transfers between devices  78.1 us (30%)
  blocking collectives  65.4 us (25%)
  local copies, waits for them, and re-layouts  64.7 us (25%)
  matrix products  20.7 us (8%)
  between operations  17.4 us (7%)
  starting transfers between devices  9.52 us (4%)
  other arithmetic  6.92 us (3%)
    psum x1, blocking collectives, body(): shrink = lax.psum(shrink, 'tp')  65.4 us
    all_gather x1, waiting for transfers between devices, body(): whole = lax.all_gather(tokens, 'tp', axis=2, tiled=True)  50.4 us
    all_to_all x1, waiting for transfers between devices, body(): lax.all_to_all(chosen(a_store), 'tp', split_axis=2, concat_axis=0, tiled=...  26.9 us
    unnamed x19, local copies, waits for them, and re-layouts  26.1 us
    all_to_all x1, local copies, waits for them, and re-layouts, body(): lax.all_to_all(chosen(a_store), 'tp', split_axis=2, concat_axis=0, tiled=...  17.8 us
    concatenate x2, local copies, waits for them, and re-layouts, chosen(): jnp.concatenate([lax.dynamic_slice_in_dim(store, mine_low, 1, 0), lax.dyn...  15.4 us
    dot_general x1, matrix products, body(): lax.dot_general(down_weight, hidden, (((0,), (1,)), ((), ())), preferred_...  9.4 us
    all_to_all x1, starting transfers between devices, body(): lax.all_to_all(chosen(a_store), 'tp', split_axis=2, concat_axis=0, tiled=...  5.94 us
  transfers between devices with their start and end apart: 4, of which 2 were waited for; matrix products, arithmetic and copies ran while one was open for 24% of the time, Pallas kernels for 0%

profile of v1, /device:TPU:0, one launch (start us, length us, event | category | flops | bytes accessed | tf_op | source)
XLA Modules:
  0.0 262.7 jit_solution(3698586607306244266)
XLA Ops:
  7.3 0.9 select_reduce_fusion
  14.0 1.0 constant_dynamic-slice_fusion.2
  15.0 50.4 %all-gather.2.cloned.1.call-done = bf16[2,256,4096]{2,1,0:T(8,128)(2,1)} async-done(((bf16[2,256,256]{2,1,0:T(8,128)(2,1)}), bf16[2,256,4096]{2,1,0:T(8,128)(2,1)}) %all-gather.2.cloned.1.call-update) | async-done | bytes 4194320 | tf_op jit(solution)/shard_map/all_gather | solution.py:49
  65.5 3.2 %multiply_reduce_fusion = f32[2,256]{1,0:T(2,128)S(1)} fusion(bf16[2,256,4096]{2,1,0:T(8,128)(2,1)} %all-gather.2.cloned.1.call-done), kind=kLoop, calls=%fused_computation.3 | loop fusion | flops 6290944 | bytes 4196352 | tf_op jit(solution)/shard_map/reduce_sum | solution.py:53
  68.9 1.7 fusion.1
  70.6 1.7 copy-done.1
  72.3 4.5 %fusion.8 = f32[512,1024]{1,0:T(8,128)S(1)} fusion(bf16[512,4096]{1,0:T(8,128)(2,1)S(1)} %fusion.1, bf16[4096,1024]{1,0:T(8,128)(2,1)S(1)} %copy-done.1), kind=kOutput, calls=%fused_computation.36 | convolution fusion | flops 4294967296 | bytes 14680064 | tf_op jit(solution)/shard_map/dot_general | solution.py:55
  76.8 4.7 %multiply_convert_fusion = bf16[512,1024]{1,0:T(8,128)(2,1)S(1)} fusion(f32[512,1024]{1,0:T(8,128)S(1)} %fusion.8, bf16[512,4096]{1,0:T(8,128)(2,1)S(1)} %fusion.1, bf16[4096,1024]{1,0:T(8,128)(2,1)S(1)} %bitcast.54), kind=kOutput, calls=%fused_computation.6 | convolution fusion | flops 4298113024 | bytes 15728640 | tf_op jit(solution)/shard_map/dot_general | solution.py:56
  81.6 1.0 copy-done.2
  82.6 9.4 %fusion.2 = bf16[4096,512]{0,1:T(8,128)(2,1)} fusion(bf16[512,1024]{1,0:T(8,128)(2,1)S(1)} %multiply_convert_fusion, bf16[1024,4096]{1,0:T(8,128)(2,1)} %param.13), kind=kOutput, calls=%fused_computation.5 | convolution fusion | flops 4297064448 | bytes 13631488 | tf_op jit(solution)/shard_map/dot_general | solution.py:72
  92.1 2.7 %copy.36 = bf16[2,16,4096]{1,0,2:T(2,128)(2,1)S(1)} copy(bf16[2,16,4096]{2,1,0:T(8,128)(2,1)S(1)} %pad_maximum_fusion.1) | data formatting | bytes 524288 | tf_op jit(solution)/shard_map/concatenate | solution.py:41
  94.8 2.8 %reshape.103 = bf16[16,2,4096]{2,1,0:T(2,128)(2,1)} reshape(bf16[4096,2,16]{2,1,0:T(2,128)(2,1)S(1)} %bitcast.45) | data formatting | bytes 524288
  97.6 3.5 %all-to-all-start = ((bf16[16,2,4096]{2,1,0:T(2,128)(2,1)}), bf16[16,2,4096]{2,1,0:T(2,128)(2,1)S(1)}, u32[]{:S(2)}, u32[]{:S(2)}) async-start(bf16[16,2,4096]{2,1,0:T(2,128)(2,1)} %reshape.103), calls=%async_computation.1 | async-start | bytes 524288 | tf_op jit(solution)/shard_map/all_to_all | solution.py:60
  101.2 1.3 constant_dynamic-slice_fusion
  102.6 12.6 %copy.39 = bf16[2,16,16384]{1,0,2:T(2,128)(2,1)} copy(bf16[2,16,16384]{2,1,0:T(8,128)(2,1)S(1)} %pad_maximum_fusion) | data formatting | bytes 2097152 | tf_op jit(solution)/shard_map/concatenate | solution.py:41
  115.2 11.3 %reshape.105 = bf16[16,2,16384]{2,1,0:T(2,128)(2,1)} reshape(bf16[16384,2,16]{2,1,0:T(2,128)(2,1)} %bitcast.43) | data formatting | bytes 2097152
  126.6 5.9 %all-to-all-start.1 = ((bf16[16,2,16384]{2,1,0:T(2,128)(2,1)}), bf16[16,2,16384]{2,1,0:T(2,128)(2,1)S(1)}, u32[]{:S(2)}, u32[]{:S(2)}) async-start(bf16[16,2,16384]{2,1,0:T(2,128)(2,1)} %reshape.105), calls=%async_computation.2 | async-start | bytes 2097152 | tf_op jit(solution)/shard_map/all_to_all | solution.py:59
  132.7 1.4 reshape.104
  134.1 1.1 copy.45
  135.2 26.9 %all-to-all-done.1 = bf16[16,2,16384]{2,1,0:T(2,128)(2,1)S(1)} async-done(((bf16[16,2,16384]{2,1,0:T(2,128)(2,1)}), bf16[16,2,16384]{2,1,0:T(2,128)(2,1)S(1)}, u32[]{:S(2)}, u32[]{:S(2)}) %all-to-all-start.1) | async-done | bytes 1048608 | tf_op jit(solution)/shard_map/all_to_all | solution.py:59
  162.1 7.5 %reshape.106 = bf16[16384,2,16]{2,1,0:T(2,128)(2,1)} reshape(bf16[16,2,16384]{2,1,0:T(2,128)(2,1)S(1)} %all-to-all-done.1) | data formatting | bytes 2097152
  169.6 17.8 %copy.40 = bf16[2,16,16,1024]{3,1,0,2:T(8,128)(2,1)S(1)} copy(bf16[2,16,16,1024]{1,0,3,2:T(2,128)(2,1)} %bitcast.44) | data formatting | bytes 2097152 | tf_op jit(solution)/shard_map/all_to_all | solution.py:59
  188.2 65.4 %psum.7 = bf16[16,512]{1,0:T(8,128)(2,1)S(1)} all-reduce(f32[16,512]{1,0:T(8,128)S(1)} %fusion.3), channel_id=1, replica_groups=mesh['rep'=2,'tp'=16] {'tp'}, use_global_device_ids=true, to_apply=%region_7.8 | all-reduce | flops 8192 | bytes 49152 | tf_op jit(solution)/shard_map/psum | solution.py:70
  253.7 1.3 fusion.5
  (34 shorter events, 5.0 us)
Async XLA Ops:
  6.5 58.9 %all-gather.2.cloned.1.call-start = ((), (), s32[]{:S(2)}) async-start(), calls=%async_computation.3 | async-start | bytes 4456448 | tf_op jit(solution)/shard_map/all_gather | solution.py:49
  7.3 246.4 %reduce-scatter.2.cloned.1.call-start = ((), (), s32[]{:S(2)}) async-start(), calls=%async_computation.4 | async-start | bytes 4456448 | tf_op jit(solution)/shard_map/reduce_scatter | solution.py:75
  65.5 3.4 %copy-start = (bf16[2,256,4096]{2,1,0:T(8,128)(2,1)S(1)}, bf16[2,256,4096]{2,1,0:T(8,128)(2,1)}, u32[]{:S(2)}) copy-start(bf16[2,256,4096]{2,1,0:T(8,128)(2,1)} %all-gather.2.cloned.1.call-done) | copy-start | bytes 12582916
  68.9 3.4 %copy-start.1 = (bf16[4096,1024]{1,0:T(8,128)(2,1)S(1)}, bf16[4096,1024]{1,0:T(8,128)(2,1)}, u32[]{:S(2)}) copy-start(bf16[4096,1024]{1,0:T(8,128)(2,1)} %param.11) | copy-start | bytes 25165828
  68.9 7.9 %slice-start = ((s8[8388608]{0:T(1024)(128)(4,1)}), s8[4194304]{0:T(1024)(128)(4,1)S(1)}, s32[]{:S(2)}) async-start(s8[8388608]{0:T(1024)(128)(4,1)} %bitcast.53), calls=%async_computation.5 | async-start | bytes 8388608
  72.3 4.5 %slice-start.1 = ((s8[8388608]{0:T(1024)(128)(4,1)}), s8[4194304]{0:T(1024)(128)(4,1)S(1)}, s32[]{:S(2)}) async-start(s8[8388608]{0:T(1024)(128)(4,1)} %bitcast.53), calls=%async_computation.6 | async-start | bytes 8388608
  81.6 1.1 copy-start.2
  97.6 29.0 %all-to-all-start = ((bf16[16,2,4096]{2,1,0:T(2,128)(2,1)}), bf16[16,2,4096]{2,1,0:T(2,128)(2,1)S(1)}, u32[]{:S(2)}, u32[]{:S(2)}) async-start(bf16[16,2,4096]{2,1,0:T(2,128)(2,1)} %reshape.103), calls=%async_computation.1 | async-start | bytes 524288 | tf_op jit(solution)/shard_map/all_to_all | solution.py:60
  126.6 35.5 %all-to-all-start.1 = ((bf16[16,2,16384]{2,1,0:T(2,128)(2,1)}), bf16[16,2,16384]{2,1,0:T(2,128)(2,1)S(1)}, u32[]{:S(2)}, u32[]{:S(2)}) async-start(bf16[16,2,16384]{2,1,0:T(2,128)(2,1)} %reshape.105), calls=%async_computation.2 | async-start | bytes 2097152 | tf_op jit(solution)/shard_map/all_to_all | solution.py:59
  169.6 17.8 %copy-start.3 = (bf16[512,1024]{1,0:T(8,128)(2,1)S(1)}, bf16[512,1024]{1,0:T(8,128)(2,1)}, u32[]{:S(2)}) copy-start(bf16[512,1024]{1,0:T(8,128)(2,1)} %copy-done.2) | copy-start | bytes 3145732
Sparse Core Ops, SparseCore 0:
  9.5 55.8 all-gather.1
  92.1 84.9 reduce-scatter.1

commit v2 on v1

--- a/solution.py
+++ b/solution.py
@@ -1,11 +1,410 @@
+import functools
+
 import jax
 import jax.numpy as jnp
 from jax import lax
+from jax.experimental import pallas as pl
+from jax.experimental.pallas import tpu as pltpu
 from jax.sharding import PartitionSpec as P
 
 EPS = 1e-06
 ADAPTER_SCALING = 2.0
 MOST = 2
+
+
+def block_kernel(
+    n,
+    x_ref,
+    gain_ref,
+    gate_ref,
+    up_ref,
+    down_ref,
+    a_ref,
+    b_ref,
+    place_ref,
+    out_ref,
+    gate_v,
+    up_v,
+    down_v,
+    squares,
+    normed,
+    gate_acc,
+    up_acc,
+    hidden,
+    a_got,
+    b_got,
+    pair_out,
+    pair_in,
+    ring_out,
+    ring_in,
+    fold_out,
+    fold_in,
+    spread,
+    final,
+    load_sem,
+    sq_send,
+    sq_recv,
+    ag_send,
+    ag_recv,
+    sib_send,
+    sib_recv,
+    a_send,
+    a_recv,
+    b_send,
+    b_recv,
+    pair_send,
+    pair_recv,
+    rs_send,
+    rs_recv,
+    fold_send,
+    fold_recv,
+):
+    chips = n // 2
+    rows, piece = x_ref.shape
+    width = n * piece
+    units = gate_v.shape[1]
+    most_rank = a_ref.shape[0]
+    rank = most_rank // MOST
+    tile = min(256, units)
+    me = lax.axis_index("tp")
+    core = me % 2
+    chip = me // 2
+
+    def place_of(c):
+        z, y = c // 2, c % 2
+        return z + y * (chips - 1 - 2 * z)
+
+    def chip_at(place):
+        y = place // (chips // 2)
+        z = place + y * (chips - 1 - 2 * place)
+        return 2 * z + y
+
+    place = place_of(chip)
+
+    def device_at(which_core, back):
+        shift = back * (1 - 2 * which_core)
+        at = (place - shift + 2 * chips) % chips
+        return 2 * chip_at(at) + which_core
+
+    sibling = me + 1 - 2 * core
+    other = 1 - core
+    following = device_at(core, -1)
+
+    def remote(src, dst, send, recv, to):
+        return pltpu.make_async_remote_copy(
+            src_ref=src,
+            dst_ref=dst,
+            send_sem=send,
+            recv_sem=recv,
+            device_id={"tp": to},
+            device_id_type=pl.DeviceIdType.MESH,
+        )
+
+    loads = [
+        pltpu.make_async_copy(gate_ref, gate_v, load_sem.at[0]),
+        pltpu.make_async_copy(up_ref, up_v, load_sem.at[1]),
+        pltpu.make_async_copy(down_ref, down_v, load_sem.at[2]),
+        pltpu.make_async_copy(
+            a_ref.at[:, pl.ds(pl.multiple_of(me * units, 128), units)], a_got.at[0], load_sem.at[3]
+        ),
+        pltpu.make_async_copy(
+            b_ref.at[:, pl.ds(pl.multiple_of(me * piece, 128), piece)], b_got.at[0], load_sem.at[4]
+        ),
+    ]
+    for load in loads:
+        load.start()
+
+    barrier = pltpu.get_barrier_semaphore()
+    for d in range(1, n):
+        pl.semaphore_signal(
+            barrier,
+            inc=1,
+            device_id={"tp": (me + d) % n},
+            device_id_type=pl.DeviceIdType.MESH,
+        )
+    pl.semaphore_wait(barrier, n - 1)
+
+    flat = x_ref[...].astype(jnp.float32)
+    partial = jnp.sum(flat * flat, axis=1, keepdims=True)
+    turned = jnp.transpose(jnp.broadcast_to(partial, (rows, 128)))
+    squares[0] = turned[0:1, :]
+    sq = [
+        remote(squares.at[0], squares.at[d], sq_send.at[d], sq_recv.at[d], (me + d) % n)
+        for d in range(1, n)
+    ]
+    for copy in sq:
+        copy.start()
+
+    def send_adapters(d):
+        to = (me + d) % n
+        first = remote(
+            a_ref.at[:, pl.ds(pl.multiple_of(to * units, 128), units)],
+            a_got.at[d],
+            a_send.at[d],
+            a_recv.at[d],
+            to,
+        )
+        second = remote(
+            b_ref.at[:, pl.ds(pl.multiple_of(to * piece, 128), piece)],
+            b_got.at[d],
+            b_send.at[d],
+            b_recv.at[d],
+            to,
+        )
+        first.start()
+        second.start()
+        return [first, second]
+
+    adapters = {}
+    ahead = 4
+    for d in range(1, 1 + ahead):
+        adapters[d] = send_adapters(d)
+
+    total = squares[0]
+    for d in range(1, n):
+        sq[d - 1].wait_recv()
+        total = total + squares[d]
+    scale = lax.rsqrt(total / width + EPS)
+    scale = jnp.transpose(jnp.broadcast_to(scale, (128, rows)))
+    for c in range(0, piece, 128):
+        part = flat[:, c : c + 128] * scale * gain_ref[:, c : c + 128].astype(jnp.float32)
+        normed[me, :, c : c + 128] = part.astype(jnp.bfloat16)
+
+    loads[0].wait()
+    loads[1].wait()
+
+    def gate_up(device, first):
+        at = pl.ds(pl.multiple_of(device * piece, 128), piece)
+
+        @pl.loop(0, units, step=tile)
+        def _(start):
+            to = pl.ds(pl.multiple_of(start, 128), tile)
+            g = jnp.dot(normed[device], gate_v[at, to], preferred_element_type=jnp.float32)
+            u = jnp.dot(normed[device], up_v[at, to], preferred_element_type=jnp.float32)
+            if first:
+                gate_acc[:, to] = g
+                up_acc[:, to] = u
+            else:
+                gate_acc[:, to] += g
+                up_acc[:, to] += u
+
+    pending = []
+    queue = list(range(1 + ahead, n))
+    for s in range(chips):
+        mine = device_at(core, s)
+        theirs = device_at(other, s)
+        if s < chips - 1:
+            ring = remote(
+                normed.at[mine], normed.at[mine], ag_send.at[s], ag_recv.at[s], following
+            )
+            ring.start()
+            pending.append(ring)
+        to_sib = remote(
+            normed.at[mine], normed.at[mine], sib_send.at[s], sib_recv.at[s], sibling
+        )
+        to_sib.start()
+        pending.append(to_sib)
+        for _ in range(2):
+            if queue:
+                d = queue.pop(0)
+                adapters[d] = send_adapters(d)
+        gate_up(mine, s == 0)
+        to_sib.wait_recv()
+        gate_up(theirs, False)
+        if s < chips - 1:
+            ring.wait_recv()
+    for copy in pending:
+        copy.wait_send()
+    for copy in sq:
+        copy.wait_send()
+
+    @pl.loop(0, units, step=128)
+    def _(start):
+        to = pl.ds(pl.multiple_of(start, 128), 128)
+        g = gate_acc[:, to]
+        hidden[:, to] = (g / (1.0 + jnp.exp(-g)) * up_acc[:, to]).astype(jnp.bfloat16)
+
+    loads[2].wait()
+
+    def base(device):
+        at = pl.ds(pl.multiple_of(device * piece, 128), piece)
+        return jnp.dot(hidden[...], down_v[:, at], preferred_element_type=jnp.float32)
+
+    def chosen(d):
+        owner = (me - d + n) % n
+        index = lax.broadcasted_iota(jnp.int32, (most_rank, rows), 0) // rank + owner * MOST
+        return index == place_ref[...]
+
+    def shrink_partial():
+        loads[3].wait()
+        loads[4].wait()
+        for d in range(1, n):
+            adapters[d][0].wait_recv()
+            adapters[d][1].wait_recv()
+
+        def add(d, result):
+            every = lax.dot_general(
+                a_got[d],
+                hidden[...],
+                (((1,), (1,)), ((), ())),
+                preferred_element_type=jnp.float32,
+            )
+            every = jnp.where(chosen(d), every, 0.0)
+            for m in range(MOST):
+                result = result + every[m * rank : (m + 1) * rank, :]
+            return result
+
+        return lax.fori_loop(0, n, add, jnp.zeros((rank, rows), jnp.float32))
+
+    stages = n.bit_length() - 1
+    folds = []
+
+    def fold_start(t):
+        bit = 1 << t
+        partner = me + bit * (1 - 2 * ((me // bit) % 2))
+        copy = remote(
+            fold_out.at[t], fold_in.at[t], fold_send.at[t], fold_recv.at[t], partner
+        )
+        copy.start()
+        folds.append(copy)
+
+    def fold_finish(t):
+        folds[t].wait_recv()
+        return fold_out[t] + fold_in[t]
+
+    pairs = []
+    rings = []
+    shrink = None
+    for s in range(chips):
+        pair_out[s] = base(device_at(other, s + 1)).astype(jnp.bfloat16)
+        pair = remote(pair_out.at[s], pair_in.at[s], pair_send.at[s], pair_recv.at[s], sibling)
+        pair.start()
+        pairs.append(pair)
+        acc = base(device_at(core, s + 1))
+        pair.wait_recv()
+        acc = acc + pair_in[s].astype(jnp.float32)
+        if s > 0:
+            rings[s - 1].wait_recv()
+            acc = acc + ring_in[s - 1].astype(jnp.float32)
+        if s < chips - 1:
+            ring_out[s] = acc.astype(jnp.bfloat16)
+            ring = remote(ring_out.at[s], ring_in.at[s], rs_send.at[s], rs_recv.at[s], following)
+            ring.start()
+            rings.append(ring)
+        if s == 0:
+            fold_out[0] = shrink_partial()
+            fold_start(0)
+        elif s <= stages:
+            shrink = fold_finish(s - 1)
+            if s < stages:
+                fold_out[s] = shrink
+                fold_start(s)
+
+    low = shrink.astype(jnp.bfloat16).astype(jnp.float32)
+    doubled = jnp.concatenate([low] * MOST, axis=0)
+    final[...] = acc
+    group = 8
+
+    @pl.loop(0, n, step=group)
+    def _(first):
+        for i in range(group):
+            part = jnp.where(chosen(first + i), doubled, 0.0)
+            spread[i * most_rank : (i + 1) * most_rank, :] = part
+        factors = b_got[pl.ds(first, group)].reshape(group * most_rank, piece)
+        left = jnp.transpose(spread[...]).astype(jnp.bfloat16)
+        final[...] += ADAPTER_SCALING * jnp.dot(
+            left, factors, preferred_element_type=jnp.float32
+        )
+
+    out_ref[...] = final[...].astype(out_ref.dtype)
+
+    for copies in adapters.values():
+        for copy in copies:
+            copy.wait_send()
+    for copy in pairs + rings + folds:
+        copy.wait_send()
+
+
+def fused(tokens, prenorm_gain, gate_matrix, up_weight, down_weight, a_sel, b_sel, place_all):
+    n = lax.axis_size("tp")
+    me = lax.axis_index("tp")
+    chips = n // 2
+    stages = n.bit_length() - 1
+    steps_count, rows_count, piece = tokens.shape
+    rows = steps_count * rows_count
+    width, units = gate_matrix.shape
+    most_rank = a_sel.shape[0]
+    rank = most_rank // MOST
+    x = tokens.reshape(rows, piece)
+    gain = lax.dynamic_slice_in_dim(prenorm_gain, me * piece, piece, 0).reshape(1, piece)
+    bf16, f32 = jnp.bfloat16, jnp.float32
+    sem = pltpu.SemaphoreType.DMA
+    vmem = pl.BlockSpec(memory_space=pltpu.VMEM)
+    anywhere = pl.BlockSpec(memory_space=pl.ANY)
+    return pl.pallas_call(
+        functools.partial(block_kernel, n),
+        out_shape=jax.ShapeDtypeStruct((rows, piece), bf16),
+        in_specs=[vmem, vmem, anywhere, anywhere, anywhere, anywhere, anywhere, vmem],
+        out_specs=vmem,
+        scratch_shapes=[
+            pltpu.VMEM((width, units), bf16),
+            pltpu.VMEM((width, units), bf16),
+            pltpu.VMEM((units, width), bf16),
+            pltpu.VMEM((n, 1, rows), f32),
+            pltpu.VMEM((n, rows, piece), bf16),
+            pltpu.VMEM((rows, units), f32),
+            pltpu.VMEM((rows, units), f32),
+            pltpu.VMEM((rows, units), bf16),
+            pltpu.VMEM((n, most_rank, units), bf16),
+            pltpu.VMEM((n, most_rank, piece), bf16),
+            pltpu.VMEM((chips, rows, piece), bf16),
+            pltpu.VMEM((chips, rows, piece), bf16),
+            pltpu.VMEM((chips - 1, rows, piece), bf16),
+            pltpu.VMEM((chips - 1, rows, piece), bf16),
+            pltpu.VMEM((stages, rank, rows), f32),
+            pltpu.VMEM((stages, rank, rows), f32),
+            pltpu.VMEM((8 * most_rank, rows), f32),
+            pltpu.VMEM((rows, piece), f32),
+            sem((5,)),
+            sem((n,)),
+            sem((n,)),
+            sem((chips,)),
+            sem((chips,)),
+            sem((chips,)),
+            sem((chips,)),
+            sem((n,)),
+            sem((n,)),
+            sem((n,)),
+            sem((n,)),
+            sem((chips,)),
+            sem((chips,)),
+            sem((chips,)),
+            sem((chips,)),
+            sem((stages,)),
+            sem((stages,)),
+        ],
+        compiler_params=pltpu.CompilerParams(
+            collective_id=0, has_side_effects=True, vmem_limit_bytes=58 * 1024 * 1024
+        ),
+        cost_estimate=pl.CostEstimate(
+            flops=6 * rows * width * units, bytes_accessed=6 * width * units, transcendentals=0
+        ),
+    )(x, gain, gate_matrix, up_weight, down_weight, a_sel, b_sel, place_all.reshape(1, rows))
+
+
+def fits(n, rows, piece, units, rank):
+    held = 3 * n * piece * units * 2 + 8 * rows * units + 2 * n * rows * piece * 2
+    return (
+        n >= 8
+        and n & (n - 1) == 0
+        and n.bit_length() - 1 < n // 2
+        and n // 2 <= 8
+        and rows % 128 == 0
+        and piece % 128 == 0
+        and units % 128 == 0
+        and rank % 16 == 0
+        and held < 48 * 1024 * 1024
+    )
 
 
 def body(
@@ -45,6 +444,21 @@
             ],
             axis=0,
         )
+
+    steps_count, rows_count, piece = tokens.shape
+    total_rows = steps_count * rows_count
+    if fits(groups, total_rows, piece, gate_matrix.shape[1], rank_count):
+        mixed = fused(
+            tokens,
+            prenorm_gain,
+            gate_matrix,
+            up_weight,
+            down_weight,
+            chosen(a_store).reshape(MOST * rank_count, hidden_all),
+            chosen(b_store).reshape(MOST * rank_count, groups * piece),
+            jnp.tile(compact, steps_count),
+        )
+        return mixed.T.reshape(piece, steps_count, rows_count)
 
     whole = lax.all_gather(tokens, "tp", axis=2, tiled=True)
     steps_count, rows_count, width = whole.shape

time: 264 us -> 132 us (0.50)
  Pallas kernels: 0 us -> 117 us
  waiting for transfers between devices: 78.1 us -> 0 us
  blocking collectives: 65.4 us -> 0 us
  local copies, waits for them, and re-layouts: 64.7 us -> 7.14 us
  matrix products: 20.7 us -> 0 us
  between operations: 17.4 us -> 3.92 us
  starting transfers between devices: 9.52 us -> 0 us
  other arithmetic: 6.92 us -> 2.91 us
    pallas_call x0 -> x1, Pallas kernels: none -> 117 us  [fused(): pl.pallas_call(functools.partial(block_kernel, n), out_shape=jax.ShapeDty...]
    psum x1 -> x0, blocking collectives: 65.4 us -> none  [body(): shrink = lax.psum(shrink, 'tp')]
    all_gather x1 -> x0, waiting for transfers between devices: 50.4 us -> none  [body(): whole = lax.all_gather(tokens, 'tp', axis=2, tiled=True)]
    all_to_all x2 -> x0, waiting for transfers between devices: 26.9 us -> none  [the longest x1 26.9 us: body(): lax.all_to_all(chosen(a_store), 'tp', split_axis=2, concat_axis=0, tiled=...]
    unnamed x19 -> x2, local copies, waits for them, and re-layouts: 26.1 us -> 0.59 us
    dot_general x5 -> x0, matrix products: 20.7 us -> none  [the longest x1 9.4 us: body(): lax.dot_general(down_weight, hidden, (((0,), (1,)), ((), ())), preferred_...]
    all_to_all x2 -> x0, local copies, waits for them, and re-layouts: 18.9 us -> none  [the longest x1 17.8 us: body(): lax.all_to_all(chosen(a_store), 'tp', split_axis=2, concat_axis=0, tiled=...]
    concatenate x2 -> x0, local copies, waits for them, and re-layouts: 15.4 us -> none  [chosen(): jnp.concatenate([lax.dynamic_slice_in_dim(store, mine_low, 1, 0), lax.dyn...]
  transfers between devices with their start and end apart: 4 -> 0, of which waited for: 2 -> 0; matrix products, arithmetic and copies ran while one was open for 24% -> 0% of each run, Pallas kernels for 0% -> 0%
where the time goes in v2:
time: 132 us; the launch traced here: 131 us
  Pallas kernels  117 us (89%)
  local copies, waits for them, and re-layouts  7.14 us (5%)
  between operations  3.92 us (3%)
  other arithmetic  2.91 us (2%)
    pallas_call x1, Pallas kernels, fused(): pl.pallas_call(functools.partial(block_kernel, n), out_shape=jax.ShapeDty...  117 us

profile of v2, /device:TPU:0, one launch (start us, length us, event | category | flops | bytes accessed | tf_op | source)
XLA Modules:
  0.0 131.4 jit_solution(16234655846083431148)
XLA Ops:
  0.0 0.9 select_reduce_fusion
  0.9 0.1 select_reduce_fusion.3
  1.0 0.6 dynamic_slice.23
  3.5 0.6 dynamic_slice.25
  6.1 1.3 constant_dynamic-slice_fusion.3
  7.4 1.1 pad_maximum_fusion
  8.4 1.0 constant_dynamic-slice_fusion.1
  9.4 0.7 pad_maximum_fusion.1
  10.2 0.1 select_reduce_fusion.1
  10.3 0.6 copy.12
  10.8 0.8 dynamic_slice.22
  11.6 0.5 reshape.48.gain_ref
  12.1 117.4 %shard_map.91 = bf16[512,256]{1,0:T(8,128)(2,1)} custom-call(bf16[512,256]{1,0:T(8,128)(2,1)} %bitcast.16, bf16[1,256]{1,0:T(2,128)(2,1)} %reshape.48.gain_ref, bf16[4096,1024]{1,0:T(8,128)(2,1)} %gate_ref.1, bf16[4096,1024]{1,0:T(8,128)(2,1)} %up_ref.1, bf16[1024,4096]{1,0:T(8,128)(2,1)} %down_ref.1, bf16[32,16384]{1,0:T(8,128)(2,1)} %bitcast.12, ...), custom_call_target="tpu_custom_call" | custom-call | flops 12884901888 | bytes 25165824 | tf_op jit(solution)/shard_map/pallas_call | solution.py:344
  129.6 1.8 %copy.11 = bf16[256,2,256]{2,1,0:T(2,128)(2,1)} copy(bf16[256,2,256]{0,2,1:T(8,128)(2,1)} %bitcast.14) | data formatting | bytes 524288 | tf_op jit(solution)/shard_map/reshape | solution.py:461
  (3 shorter events, 0.0 us)

commit v3 on v2

--- a/solution.py
+++ b/solution.py
@@ -10,6 +10,7 @@
 EPS = 1e-06
 ADAPTER_SCALING = 2.0
 MOST = 2
+PARTS = 8
 
 
 def block_kernel(
@@ -100,18 +101,25 @@
             device_id_type=pl.DeviceIdType.MESH,
         )
 
+    weights = []
+    for w, (source, held) in enumerate(((gate_ref, gate_v), (up_ref, up_v), (down_ref, down_v))):
+        share = source.shape[0] // PARTS
+        for i in range(PARTS):
+            span = pl.ds(i * share, share)
+            weights.append(
+                pltpu.make_async_copy(
+                    source.at[span, :], held.at[span, :], load_sem.at[2 + w * PARTS + i]
+                )
+            )
     loads = [
-        pltpu.make_async_copy(gate_ref, gate_v, load_sem.at[0]),
-        pltpu.make_async_copy(up_ref, up_v, load_sem.at[1]),
-        pltpu.make_async_copy(down_ref, down_v, load_sem.at[2]),
         pltpu.make_async_copy(
-            a_ref.at[:, pl.ds(pl.multiple_of(me * units, 128), units)], a_got.at[0], load_sem.at[3]
+            a_ref.at[:, pl.ds(pl.multiple_of(me * units, 128), units)], a_got.at[0], load_sem.at[0]
         ),
         pltpu.make_async_copy(
-            b_ref.at[:, pl.ds(pl.multiple_of(me * piece, 128), piece)], b_got.at[0], load_sem.at[4]
+            b_ref.at[:, pl.ds(pl.multiple_of(me * piece, 128), piece)], b_got.at[0], load_sem.at[1]
         ),
     ]
-    for load in loads:
+    for load in weights + loads:
         load.start()
 
     barrier = pltpu.get_barrier_semaphore()
@@ -156,7 +164,7 @@
         return [first, second]
 
     adapters = {}
-    ahead = 4
+    ahead = 0
     for d in range(1, 1 + ahead):
         adapters[d] = send_adapters(d)
 
@@ -167,11 +175,13 @@
     scale = lax.rsqrt(total / width + EPS)
     scale = jnp.transpose(jnp.broadcast_to(scale, (128, rows)))
     for c in range(0, piece, 128):
-        part = flat[:, c : c + 128] * scale * gain_ref[:, c : c + 128].astype(jnp.float32)
+        part = flat[:, c : c + 128] * scale * gain_ref[
+            :, pl.ds(pl.multiple_of(me * piece + c, 128), 128)
+        ].astype(jnp.float32)
         normed[me, :, c : c + 128] = part.astype(jnp.bfloat16)
 
-    loads[0].wait()
-    loads[1].wait()
+    for load in weights[: 2 * PARTS]:
+        load.wait()
 
     def gate_up(device, first):
         at = pl.ds(pl.multiple_of(device * piece, 128), piece)
@@ -192,7 +202,6 @@
     queue = list(range(1 + ahead, n))
     for s in range(chips):
         mine = device_at(core, s)
-        theirs = device_at(other, s)
         if s < chips - 1:
             ring = remote(
                 normed.at[mine], normed.at[mine], ag_send.at[s], ag_recv.at[s], following
@@ -208,11 +217,15 @@
             if queue:
                 d = queue.pop(0)
                 adapters[d] = send_adapters(d)
+        if s > 0:
+            before.wait_recv()
+            gate_up(device_at(other, s - 1), False)
         gate_up(mine, s == 0)
-        to_sib.wait_recv()
-        gate_up(theirs, False)
+        before = to_sib
         if s < chips - 1:
             ring.wait_recv()
+    before.wait_recv()
+    gate_up(device_at(other, chips - 1), False)
     for copy in pending:
         copy.wait_send()
     for copy in sq:
@@ -224,7 +237,8 @@
         g = gate_acc[:, to]
         hidden[:, to] = (g / (1.0 + jnp.exp(-g)) * up_acc[:, to]).astype(jnp.bfloat16)
 
-    loads[2].wait()
+    for load in weights[2 * PARTS :]:
+        load.wait()
 
     def base(device):
         at = pl.ds(pl.multiple_of(device * piece, 128), piece)
@@ -236,25 +250,30 @@
         return index == place_ref[...]
 
     def shrink_partial():
-        loads[3].wait()
-        loads[4].wait()
+        loads[0].wait()
+        loads[1].wait()
         for d in range(1, n):
             adapters[d][0].wait_recv()
             adapters[d][1].wait_recv()
 
-        def add(d, result):
+        group = n // 2
+        half = group * most_rank
+
+        def add(g, result):
             every = lax.dot_general(
-                a_got[d],
+                a_got[pl.ds(g * group, group)].reshape(half, units),
                 hidden[...],
                 (((1,), (1,)), ((), ())),
                 preferred_element_type=jnp.float32,
             )
-            every = jnp.where(chosen(d), every, 0.0)
-            for m in range(MOST):
-                result = result + every[m * rank : (m + 1) * rank, :]
+            for i in range(group):
+                part = every[i * most_rank : (i + 1) * most_rank, :]
+                part = jnp.where(chosen(g * group + i), part, 0.0)
+                for m in range(MOST):
+                    result = result + part[m * rank : (m + 1) * rank, :]
             return result
 
-        return lax.fori_loop(0, n, add, jnp.zeros((rank, rows), jnp.float32))
+        return lax.fori_loop(0, 2, add, jnp.zeros((rank, rows), jnp.float32))
 
     stages = n.bit_length() - 1
     folds = []
@@ -275,13 +294,20 @@
     pairs = []
     rings = []
     shrink = None
-    for s in range(chips):
+    late = chips - 1 - stages
+
+    def pair_start(s):
         pair_out[s] = base(device_at(other, s + 1)).astype(jnp.bfloat16)
         pair = remote(pair_out.at[s], pair_in.at[s], pair_send.at[s], pair_recv.at[s], sibling)
         pair.start()
         pairs.append(pair)
+
+    pair_start(0)
+    for s in range(chips):
+        if s < chips - 1:
+            pair_start(s + 1)
         acc = base(device_at(core, s + 1))
-        pair.wait_recv()
+        pairs[s].wait_recv()
         acc = acc + pair_in[s].astype(jnp.float32)
         if s > 0:
             rings[s - 1].wait_recv()
@@ -291,14 +317,15 @@
             ring = remote(ring_out.at[s], ring_in.at[s], rs_send.at[s], rs_recv.at[s], following)
             ring.start()
             rings.append(ring)
-        if s == 0:
+        t = s - late
+        if t == 0:
             fold_out[0] = shrink_partial()
             fold_start(0)
-        elif s <= stages:
-            shrink = fold_finish(s - 1)
-            if s < stages:
-                fold_out[s] = shrink
-                fold_start(s)
+        elif t > 0:
+            shrink = fold_finish(t - 1)
+            if t < stages:
+                fold_out[t] = shrink
+                fold_start(t)
 
     low = shrink.astype(jnp.bfloat16).astype(jnp.float32)
     doubled = jnp.concatenate([low] * MOST, axis=0)
@@ -325,9 +352,56 @@
         copy.wait_send()
 
 
+def select_kernel(n, slot_ref, row_ref, a_ref, b_ref, a_out, b_out, place_ref, sem):
+    held, rank, _ = a_ref.shape
+    adapters = slot_ref.shape[1]
+    rows = row_ref.shape[1]
+    me = lax.axis_index("tp")
+    slots = jnp.transpose(jnp.broadcast_to(slot_ref[...], (adapters, adapters)))[:, 0:1]
+    named = lax.broadcasted_iota(jnp.int32, (adapters, rows), 0) == row_ref[...]
+    row_slot = jnp.sum(jnp.where(named, slots, 0), axis=0, keepdims=True)
+    home = row_slot // held
+    local = row_slot - home * held
+    at_home = lax.broadcasted_iota(jnp.int32, (n, rows), 0) == home
+    lowest = jnp.min(jnp.where(at_home, local, held - 1), axis=1, keepdims=True)
+    row_lowest = jnp.sum(jnp.where(at_home, lowest, 0), axis=0, keepdims=True)
+    place = home * MOST + (local != row_lowest).astype(jnp.int32)
+    for start in range(0, place_ref.shape[1], rows):
+        place_ref[:, start : start + rows] = place
+    low = jnp.min(jnp.where(home == me, local, held - 1))
+    high = jnp.max(jnp.where(home == me, local, 0))
+    copies = []
+    for i, at in enumerate((low, high)):
+        to = pl.ds(i * rank, rank)
+        copies.append(pltpu.make_async_copy(a_ref.at[at], a_out.at[to, :], sem.at[2 * i]))
+        copies.append(pltpu.make_async_copy(b_ref.at[at], b_out.at[to, :], sem.at[2 * i + 1]))
+    for copy in copies:
+        copy.start()
+    for copy in copies:
+        copy.wait()
+
+
+def select(adapter_slot, row_adapter, a_store, b_store, steps_count):
+    n = lax.axis_size("tp")
+    rank = a_store.shape[1]
+    rows = row_adapter.shape[0]
+    vmem = pl.BlockSpec(memory_space=pltpu.VMEM)
+    anywhere = pl.BlockSpec(memory_space=pl.ANY)
+    return pl.pallas_call(
+        functools.partial(select_kernel, n),
+        out_shape=(
+            jax.ShapeDtypeStruct((MOST * rank, a_store.shape[2]), a_store.dtype),
+            jax.ShapeDtypeStruct((MOST * rank, b_store.shape[2]), b_store.dtype),
+            jax.ShapeDtypeStruct((1, steps_count * rows), jnp.int32),
+        ),
+        in_specs=[vmem, vmem, anywhere, anywhere],
+        out_specs=(vmem, vmem, vmem),
+        scratch_shapes=[pltpu.SemaphoreType.DMA((2 * MOST,))],
+    )(adapter_slot.reshape(1, -1), row_adapter.reshape(1, -1), a_store, b_store)
+
+
 def fused(tokens, prenorm_gain, gate_matrix, up_weight, down_weight, a_sel, b_sel, place_all):
     n = lax.axis_size("tp")
-    me = lax.axis_index("tp")
     chips = n // 2
     stages = n.bit_length() - 1
     steps_count, rows_count, piece = tokens.shape
@@ -336,7 +410,7 @@
     most_rank = a_sel.shape[0]
     rank = most_rank // MOST
     x = tokens.reshape(rows, piece)
-    gain = lax.dynamic_slice_in_dim(prenorm_gain, me * piece, piece, 0).reshape(1, piece)
+    gain = prenorm_gain.reshape(1, width)
     bf16, f32 = jnp.bfloat16, jnp.float32
     sem = pltpu.SemaphoreType.DMA
     vmem = pl.BlockSpec(memory_space=pltpu.VMEM)
@@ -344,7 +418,7 @@
     return pl.pallas_call(
         functools.partial(block_kernel, n),
         out_shape=jax.ShapeDtypeStruct((rows, piece), bf16),
-        in_specs=[vmem, vmem, anywhere, anywhere, anywhere, anywhere, anywhere, vmem],
+        in_specs=[vmem, vmem, anywhere, anywhere, anywhere, vmem, vmem, vmem],
         out_specs=vmem,
         scratch_shapes=[
             pltpu.VMEM((width, units), bf16),
@@ -365,7 +439,7 @@
             pltpu.VMEM((stages, rank, rows), f32),
             pltpu.VMEM((8 * most_rank, rows), f32),
             pltpu.VMEM((rows, piece), f32),
-            sem((5,)),
+            sem((2 + 3 * PARTS,)),
             sem((n,)),
             sem((n,)),
             sem((chips,)),
@@ -399,7 +473,7 @@
         and n & (n - 1) == 0
         and n.bit_length() - 1 < n // 2
         and n // 2 <= 8
-        and rows % 128 == 0
+        and rows % 256 == 0
         and piece % 128 == 0
         and units % 128 == 0
         and rank % 16 == 0
@@ -421,6 +495,16 @@
     held, rank_count, hidden_all = a_store.shape
     groups = lax.axis_size("tp")
     myself = lax.axis_index("tp")
+    steps_count, rows_count, piece = tokens.shape
+    total_rows = steps_count * rows_count
+    lined = rows_count % 128 == 0 and adapter_slot.shape[0] % 128 == 0
+    if lined and fits(groups, total_rows, piece, gate_matrix.shape[1], rank_count):
+        a_sel, b_sel, places = select(adapter_slot, row_adapter, a_store, b_store, steps_count)
+        mixed = fused(
+            tokens, prenorm_gain, gate_matrix, up_weight, down_weight, a_sel, b_sel, places
+        )
+        return mixed.T.reshape(piece, steps_count, rows_count)
+
     stored = groups * held
     catalog = jnp.arange(stored, dtype=jnp.int32)
     matches = row_adapter[:, None] == catalog[None, :]
@@ -444,21 +528,6 @@
             ],
             axis=0,
         )
-
-    steps_count, rows_count, piece = tokens.shape
-    total_rows = steps_count * rows_count
-    if fits(groups, total_rows, piece, gate_matrix.shape[1], rank_count):
-        mixed = fused(
-            tokens,
-            prenorm_gain,
-            gate_matrix,
-            up_weight,
-            down_weight,
-            chosen(a_store).reshape(MOST * rank_count, hidden_all),
-            chosen(b_store).reshape(MOST * rank_count, groups * piece),
-            jnp.tile(compact, steps_count),
-        )
-        return mixed.T.reshape(piece, steps_count, rows_count)
 
     whole = lax.all_gather(tokens, "tp", axis=2, tiled=True)
     steps_count, rows_count, width = whole.shape

time: 132 us -> 120 us (0.909)
  local copies, waits for them, and re-layouts: 7.14 us -> 3.12 us
  between operations: 3.92 us -> 0.02 us
  other arithmetic: 2.91 us -> 0 us
    pallas_call x1, Pallas kernels: 117 us -> 113 us  [fused(): pl.pallas_call(functools.partial(block_kernel, n), out_shape=jax.ShapeDty...]
    dynamic_slice x5 -> x0, local copies, waits for them, and re-layouts: 4.19 us -> none  [the longest x2 2.26 us: chosen(): lax.dynamic_slice_in_dim(store, mine_low, 1, 0)]
    pallas_call x0 -> x1, Pallas kernels: none -> 3.44 us  [select(): pl.pallas_call(functools.partial(select_kernel, n), out_shape=(jax.ShapeD...]
    concatenate x2 -> x0, other arithmetic: 1.81 us -> none  [chosen(): jnp.concatenate([lax.dynamic_slice_in_dim(store, mine_low, 1, 0), lax.dyn...]
where the time goes in v3:
time: 120 us; the launch traced here: 119 us
  Pallas kernels  116 us (97%)
  local copies, waits for them, and re-layouts  3.12 us (3%)
    pallas_call x1, Pallas kernels, fused(): pl.pallas_call(functools.partial(block_kernel, n), out_shape=jax.ShapeDty...  113 us
    pallas_call x1, Pallas kernels, select(): pl.pallas_call(functools.partial(select_kernel, n), out_shape=(jax.ShapeD...  3.44 us

profile of v3, /device:TPU:0, one launch (start us, length us, event | category | flops | bytes accessed | tf_op | source)
XLA Modules:
  0.0 119.4 jit_solution(8360063059174576393)
XLA Ops:
  0.0 1.3 %reshape.16.gain_ref = bf16[1,4096]{1,0:T(2,128)(2,1)} reshape(bf16[4096]{0:T(1024)(128)(2,1)} %param.10) | data formatting | bytes 16384 | tf_op jit(solution)/shard_map/reshape | solution.py:413
  1.3 3.4 %shard_map.91 = (bf16[32,16384]{1,0:T(8,128)(2,1)}, bf16[32,4096]{1,0:T(8,128)(2,1)}, s32[1,512]{1,0:T(1,128)}) custom-call(s32[1,128]{1,0:T(1,128)} %bitcast.8, s32[1,256]{1,0:T(1,128)} %bitcast.7, bf16[8,16,16384]{2,1,0:T(8,128)(2,1)} %a_ref.1, bf16[8,16,4096]{2,1,0:T(8,128)(2,1)} %b_ref.1), custom_call_target="tpu_custom_call" | custom-call | tf_op jit(solution)/shard_map/pallas_call | solution.py:390
  4.8 112.8 %shard_map.92 = bf16[512,256]{1,0:T(8,128)(2,1)} custom-call(bf16[512,256]{1,0:T(8,128)(2,1)} %bitcast.9, bf16[1,4096]{1,0:T(2,128)(2,1)} %reshape.16.gain_ref, bf16[4096,1024]{1,0:T(8,128)(2,1)} %gate_ref.1, bf16[4096,1024]{1,0:T(8,128)(2,1)} %up_ref.1, bf16[1024,4096]{1,0:T(8,128)(2,1)} %down_ref.1, bf16[32,16384]{1,0:T(8,128)(2,1)} %get-tuple-element.8.a_ref, ...), custom_call_target="tpu_custom_call" | custom-call | flops 12884901888 | bytes 25165824 | tf_op jit(solution)/shard_map/pallas_call | solution.py:418
  117.6 1.8 %copy.10 = bf16[256,2,256]{2,1,0:T(2,128)(2,1)} copy(bf16[256,2,256]{0,2,1:T(8,128)(2,1)} %bitcast.6) | data formatting | bytes 524288 | tf_op jit(solution)/shard_map/reshape | solution.py:506
